TPU v7x, 128 devices: a whole 4x4x4 slice. The times are simulated.
128 devices in a mesh: dp: 8 (over x, core), mp: 16 (over y, z).
Axes of the slice: x: 4, y: 4, z: 4, core: 2. Of those that a mesh axis runs over, the one named last changes fastest.
Arguments:
- tokens: bfloat16 [16384, 1024], P(('dp', 'mp')), may hold values from -6 to 6
- lengths: int32 [8], P('dp'), may hold values from 1024 to 2048, as said below
- cotangent: bfloat16 [16384, 1024], P(('dp', 'mp')), may hold values from -6 to 6
- norm_one: float32 [1024], replicated, may hold values from 0.5 to 1.5
- recur_input: bfloat16 [1024, 1536], P(None, 'mp'), may hold values from -0.1875 to 0.1875
- recur_gate: bfloat16 [1024, 1536], P(None, 'mp'), may hold values from -0.1875 to 0.1875
- conv_kernel: float32 [4, 1536], P(None, 'mp'), may hold values from -3 to 3
- conv_bias: float32 [1536], P('mp'), may hold values from -3 to 3
- decay_gate: float32 [16, 96, 96], P('mp'), may hold values from -0.625 to 0.625
- decay_shift: float32 [1536], P('mp'), may hold values from -4 to 4
- input_gate: float32 [16, 96, 96], P('mp'), may hold values from -0.625 to 0.625
- input_shift: float32 [1536], P('mp'), may hold values from -4 to 4
- decay_param: float32 [1536], P('mp'), may hold values from 3.5 to 14
- recur_output: bfloat16 [1536, 1024], P('mp'), may hold values from -0.4375 to 0.4375
- norm_two: float32 [1024], replicated, may hold values from 0.5 to 1.5
- first_gate: bfloat16 [1024, 3072], P('dp', 'mp'), may hold values from -0.1875 to 0.1875
- first_value: bfloat16 [1024, 3072], P('dp', 'mp'), may hold values from -0.1875 to 0.1875
- first_down: bfloat16 [3072, 1024], P('mp', 'dp'), may hold values from -0.21875 to 0.21875
- norm_three: float32 [1024], replicated, may hold values from 0.5 to 1.5
- query_proj: bfloat16 [1024, 1024], P(('dp', 'mp')), may hold values from -0.1875 to 0.1875
- key_proj: bfloat16 [1024, 128], P(('dp', 'mp')), may hold values from -0.1875 to 0.1875
- value_proj: bfloat16 [1024, 128], P(('dp', 'mp')), may hold values from -0.1875 to 0.1875
- attn_output: bfloat16 [1024, 1024], P(('dp', 'mp')), may hold values from -0.75 to 0.75
- norm_four: float32 [1024], replicated, may hold values from 0.5 to 1.5
- second_gate: bfloat16 [1024, 3072], P('dp', 'mp'), may hold values from -0.1875 to 0.1875
- second_value: bfloat16 [1024, 3072], P('dp', 'mp'), may hold values from -0.1875 to 0.1875
- second_down: bfloat16 [3072, 1024], P('mp', 'dp'), may hold values from -0.21875 to 0.21875
Outputs:
- outputs: float32 [16384, 1024], P(('dp', 'mp'))
- grad_tokens: float32 [16384, 1024], P(('dp', 'mp'))
- grad_norm_one: float32 [1024], replicated
- grad_recur_input: float32 [1024, 1536], P(None, 'mp')
- grad_recur_gate: float32 [1024, 1536], P(None, 'mp')
- grad_conv_kernel: float32 [4, 1536], P(None, 'mp')
- grad_conv_bias: float32 [1536], P('mp')
- grad_decay_gate: float32 [16, 96, 96], P('mp')
- grad_decay_shift: float32 [1536], P('mp')
- grad_input_gate: float32 [16, 96, 96], P('mp')
- grad_input_shift: float32 [1536], P('mp')
- grad_decay_param: float32 [1536], P('mp')
- grad_recur_output: float32 [1536, 1024], P('mp')
- grad_norm_two: float32 [1024], replicated
- grad_first_gate: float32 [1024, 3072], P('dp', 'mp')
- grad_first_value: float32 [1024, 3072], P('dp', 'mp')
- grad_first_down: float32 [3072, 1024], P('mp', 'dp')
- grad_norm_three: float32 [1024], replicated
- grad_query_proj: float32 [1024, 1024], P(('dp', 'mp'))
- grad_key_proj: float32 [1024, 128], P(('dp', 'mp'))
- grad_value_proj: float32 [1024, 128], P(('dp', 'mp'))
- grad_attn_output: float32 [1024, 1024], P(('dp', 'mp'))
- grad_norm_four: float32 [1024], replicated
- grad_second_gate: float32 [1024, 3072], P('dp', 'mp')
- grad_second_value: float32 [1024, 3072], P('dp', 'mp')
- grad_second_down: float32 [3072, 1024], P('mp', 'dp')
Inputs may be any that keep to these rules, and one draw needn't show every extreme that they name: lengths[g] tokens of group g form its first document, the other 2048 - lengths[g] its second one (none if lengths[g] = 2048).
All inputs are finite; a program needn't handle non-finite values.
Results may differ from a plain program's by a relative error of at most 0.02.
Values may be sent and summed in bfloat16 or wider, within the bound.
A program may use at most 192 MiB of HBM per device.

v0:
```python
import math
from types import SimpleNamespace

import jax
import jax.numpy as jnp
from jax import lax
from jax.experimental import pallas as pl
from jax.experimental.pallas import tpu as pltpu
from jax.sharding import PartitionSpec as P

MESH = pl.DeviceIdType.MESH
F32 = jnp.float32
BF16 = jnp.bfloat16
VMEM_BYTES = 63 * 2**20

D = 1024
ROWS = 128
SPAN = 512
LANE = 128
BW = 96
CH = 4 * LANE
PAR = 208
VEC = 192
UNITS = 768
HEADS = 8
HD = 128
WINDOW = 1024
KEYS = 1152
PAIR = 1152
CHUNK = 64
STEPS = ((0,), (1, 3), (2,))
HALVES = ((1, 3), (2, 0))
GELU_C = math.sqrt(2.0 / math.pi)


def place():
    dp, mp = lax.axis_index("dp"), lax.axis_index("mp")
    return dp // 2, dp % 2, mp // 4, mp % 4


def z_peer(d):
    _, _, y, z = place()
    return {"mp": y * 4 + (z + d) % 4}


def y_peer(d):
    _, _, y, z = place()
    return {"mp": ((y + d) % 4) * 4 + z}


def xc_peer(dx, dc):
    x, c, _, _ = place()
    return {"dp": ((x + dx) % 4) * 2 + (c + dc) % 2}


def row_peer(offset):
    return {"mp": lax.rem(lax.axis_index("mp") + 16 + offset, 16)}


def all_peers(window):
    peers = [xc_peer(0, 1)] + [xc_peer(d, 0) for d in (1, 2, 3)]
    if window:
        return peers + [row_peer(o) for o in range(1, 16)]
    for d in (1, 2, 3):
        peers += [y_peer(d), z_peer(d)]
    return peers


def greet(peers):
    barrier = pltpu.get_barrier_semaphore()
    for peer in peers:
        pl.semaphore_signal(barrier, inc=1, device_id=peer, device_id_type=MESH)
    return lambda: pl.semaphore_wait(barrier, len(peers))


class Net:
    def __init__(self, send, recv):
        self.send, self.recv, self.used, self.started = send, recv, 0, []
        self.landing = {}

    def make(self, src, dst, peer, shared=None):
        landing = self.landing.setdefault(shared, self.used) if shared else self.used
        copy = pltpu.make_async_remote_copy(
            src_ref=src,
            dst_ref=dst,
            send_sem=self.send.at[self.used],
            recv_sem=self.recv.at[landing],
            device_id=peer,
            device_id_type=MESH,
        )
        self.used += 1
        return copy

    def push(self, src, dst, peer):
        copy = self.make(src, dst, peer)
        copy.start()
        self.started.append(copy)
        return copy

    def drain(self):
        for copy in self.started:
            copy.wait_send()


class Local:
    def __init__(self, sems):
        self.sems, self.used, self.stores = sems, 0, []

    def load(self, src, dst):
        copy = pltpu.make_async_copy(src, dst, self.sems.at[self.used])
        self.used += 1
        copy.start()
        return copy

    def store(self, src, dst):
        self.stores.append(self.load(src, dst))

    def drain(self):
        for copy in self.stores:
            copy.wait()


def run(body, ins, outs, scratch, collective_id=None, flops=0):
    names = [n for n, _, _ in ins] + [n for n, _, _, _ in outs] + [n for n, _ in scratch]
    space = {"near": pltpu.VMEM, "far": pl.ANY}

    def kernel(*refs):
        body(SimpleNamespace(**dict(zip(names, refs))))

    results = pl.pallas_call(
        kernel,
        out_shape=[jax.ShapeDtypeStruct(s, t) for _, s, t, _ in outs],
        in_specs=[pl.BlockSpec(memory_space=space[where]) for _, _, where in ins],
        out_specs=[pl.BlockSpec(memory_space=space[where]) for _, _, _, where in outs],
        scratch_shapes=[s for _, s in scratch],
        compiler_params=pltpu.CompilerParams(
            collective_id=collective_id,
            has_side_effects=collective_id is not None,
            vmem_limit_bytes=VMEM_BYTES,
        ),
        cost_estimate=pl.CostEstimate(flops=flops, bytes_accessed=2**24, transcendentals=0),
    )(*[a for _, a, _ in ins])
    return dict(zip([n for n, _, _, _ in outs], results))


def vm(shape, dtype):
    return pltpu.VMEM(shape, dtype)


def dma(n):
    return pltpu.SemaphoreType.DMA((n,))


def dot_nn(a, b, **kw):
    return lax.dot_general(a, b, (((1,), (0,)), ((), ())), preferred_element_type=F32, **kw)


def dot_nt(a, b, **kw):
    return lax.dot_general(a, b, (((1,), (1,)), ((), ())), preferred_element_type=F32, **kw)


def dot_tn(a, b, **kw):
    return lax.dot_general(a, b, (((0,), (0,)), ((), ())), preferred_element_type=F32, **kw)


def gelu(v):
    return 0.5 * v * (1.0 + jnp.tanh(GELU_C * (v + 0.044715 * v * v * v)))


def gelu_both(v):
    t = jnp.tanh(GELU_C * (v + 0.044715 * v * v * v))
    value = 0.5 * v * (1.0 + t)
    slope = 0.5 * (1.0 + t) + 0.5 * v * (1.0 - t * t) * GELU_C * (1.0 + 3.0 * 0.044715 * v * v)
    return value, slope


def rms(v, gain):
    return v * lax.rsqrt(jnp.mean(v * v, axis=-1, keepdims=True) + 1e-06) * gain


def rms_back(dn, v, gain):
    r = lax.rsqrt(jnp.mean(v * v, axis=-1, keepdims=True) + 1e-06)
    grad_gain = jnp.sum(dn * v * r, axis=0, keepdims=True)
    dg = dn * gain
    dv = r * dg - v * (r * r * r) * jnp.mean(dg * v, axis=-1, keepdims=True)
    return dv, grad_gain


def stack(ref, slots):
    return jnp.concatenate([ref[s] for s in slots], axis=0) if len(slots) > 1 else ref[slots[0]]


def block(value, i):
    return value[i * ROWS : (i + 1) * ROWS]


def low_dot(left, right, dims):
    return lax.dot_general(
        left.astype(BF16), right.astype(BF16), (dims, ((), ())), preferred_element_type=F32
    )


def rows_at(first, count):
    return pl.ds(pl.multiple_of(first, count), count)


class Gatherer:
    def __init__(self, net, own, whole):
        self.net, self.own, self.whole, self.half = net, own, whole, whole.shape[3] // 2

    def start(self):
        x, c, y, _ = place()
        one, two = slice(0, self.half), slice(self.half, 2 * self.half)
        self.whole[c, x, y] = self.own[...]
        self.first = []
        for d in (1, 3, 2):
            for part, peer in ((one, xc_peer(d, 0)), (two, y_peer(d))):
                self.first.append(
                    self.net.push(self.own.at[part, :], self.whole.at[c, x, y, part, :], peer)
                )

    def along(self):
        x, c, y, _ = place()
        one, two = slice(0, self.half), slice(self.half, 2 * self.half)
        for copy in self.first:
            copy.wait_recv()
        self.second = []
        for d in (1, 3, 2):
            mine = self.whole.at[c, :, y, one, :]
            self.second.append(self.net.push(mine, mine, y_peer(d)))
            mine = self.whole.at[c, x, :, two, :]
            self.second.append(self.net.push(mine, mine, xc_peer(d, 0)))

    def across(self):
        _, c, _, _ = place()
        for copy in self.second:
            copy.wait_recv()
        mine = self.whole.at[c]
        self.third = self.net.push(mine, mine, xc_peer(0, 1))

    def finish(self):
        self.third.wait_recv()


class Reducer:
    @staticmethod
    def scratch(name, rows, lanes):
        half = rows // 2
        return [
            (name + "_other", vm((4, 4, rows, lanes), BF16)),
            (name + "_in_a", vm((3, 4, half, lanes), BF16)),
            (name + "_in_b", vm((3, 4, half, lanes), BF16)),
            (name + "_sum_a", vm((4, half, lanes), BF16)),
            (name + "_sum_b", vm((4, half, lanes), BF16)),
            (name + "_last_a", vm((3, half, lanes), BF16)),
            (name + "_last_b", vm((3, half, lanes), BF16)),
        ]

    def __init__(self, net, src, r, name):
        self.net, self.src, self.half = net, src, src.shape[3] // 2
        for part in ("other", "in_a", "in_b", "sum_a", "sum_b", "last_a", "last_b"):
            setattr(self, part, getattr(r, name + "_" + part))

    def start(self):
        _, c, _, _ = place()
        self.first = self.net.push(self.src.at[1 - c], self.other, xc_peer(0, 1))

    def along_one(self):
        x, c, y, _ = place()
        half = self.half
        self.first.wait_recv()

        def add(i, _):
            a, b = i // 4, i % 4
            total = self.src[c, a, b].astype(F32) + self.other[a, b].astype(F32)
            self.other[a, b] = total.astype(BF16)
            return 0

        lax.fori_loop(0, 16, add, 0)
        self.second = []
        for d in (1, 3, 2):
            mine = self.other.at[(x + d) % 4, :, 0:half, :]
            self.second.append(self.net.push(mine, self.in_a.at[d - 1], xc_peer(d, 0)))
            mine = self.other.at[:, (y + d) % 4, half : 2 * half, :]
            self.second.append(self.net.push(mine, self.in_b.at[d - 1], y_peer(d)))

    def along_two(self):
        x, _, y, _ = place()
        half = self.half
        for copy in self.second:
            copy.wait_recv()

        def add(i, _):
            a = self.other[x, i, 0:half, :].astype(F32)
            b = self.other[i, y, half : 2 * half, :].astype(F32)
            for d in range(3):
                a = a + self.in_a[d, i].astype(F32)
                b = b + self.in_b[d, i].astype(F32)
            self.sum_a[i] = a.astype(BF16)
            self.sum_b[i] = b.astype(BF16)
            return 0

        lax.fori_loop(0, 4, add, 0)
        self.third = []
        for d in (1, 3, 2):
            mine = self.sum_a.at[(y + d) % 4]
            self.third.append(self.net.push(mine, self.last_a.at[d - 1], y_peer(d)))
            mine = self.sum_b.at[(x + d) % 4]
            self.third.append(self.net.push(mine, self.last_b.at[d - 1], xc_peer(d, 0)))

    def finish(self):
        x, _, y, _ = place()
        for copy in self.third:
            copy.wait_recv()
        a = self.sum_a[y].astype(F32)
        b = self.sum_b[x].astype(F32)
        for d in range(3):
            a = a + self.last_a[d].astype(F32)
            b = b + self.last_b[d].astype(F32)
        return a, b


def spread_z(net, ref):
    z = place()[3]
    return {d: net.push(ref.at[z], ref.at[z], z_peer(d)) for d in (1, 3, 2)}


def place_units(local, whole, w_ref):
    copies = []
    for part in range(8):
        for y in range(4):
            for w in range(3):
                copies.append(
                    local.load(
                        whole.at[part % 2, part // 2, y, w * 192 : (w + 1) * 192, :],
                        w_ref.at[
                            w, y * 192 : (y + 1) * 192, part * LANE : (part + 1) * LANE
                        ],
                    )
                )
    return copies


def unit_grads(sides, out):
    for w, (left, right) in enumerate(sides):
        right = right[...].reshape(SPAN, D)
        for tile in range(3):
            cut = left[:, :, tile * 256 : tile * 256 + 256].reshape(SPAN, 256)
            grad = dot_tn(cut, right)
            first = tile * 256
            while first < tile * 256 + 256:
                block = first // 192
                last = min((block + 1) * 192, tile * 256 + 256)
                rows = grad[first - tile * 256 : last - tile * 256]
                start = w * 192 + first - block * 192
                for part in range(8):
                    out[part % 2, part // 2, block, start : start + last - first, :] = rows[
                        :, part * LANE : (part + 1) * LANE
                    ].astype(BF16)
                first = last


def positions(length, first, rows):
    t = lax.broadcasted_iota(jnp.int32, (rows, CH), 0) + first
    wide = jnp.concatenate([length[...]] * 4, axis=1)
    return jnp.where(t >= wide, t - wide, t)


def lanes_of(pr, row):
    return jnp.concatenate([pr[b, row : row + 1, :] for b in range(4)], axis=1)


def neg_expm1(v):
    series = v * (
        1.0 + v * (0.5 + v * (1.0 / 6 + v * (1.0 / 24 + v * (1.0 / 120 + v * (1.0 / 720)))))
    )
    return -jnp.where(v > -0.25, series, jnp.exp(v) - 1.0)


def share_edges(net, edges, prod, last):
    y = place()[2]
    edges[y, 0:1, :] = prod
    edges[y, 1:2, :] = last
    return [net.push(edges.at[y], edges.at[y], y_peer(d)) for d in (1, 3, 2)]


def forward_body(r):
    x, c, y, z = place()
    mp = lax.axis_index("mp")
    ready = greet(all_peers(True))
    net, loc = Net(r.send, r.recv), Local(r.sems)

    tokens = r.tok[...].astype(F32)
    r.n1[z] = rms(tokens, r.gain_one[...]).astype(BF16)
    mine = pl.ds(pl.multiple_of(y * LANE, LANE), BW)
    r.wr[0, mine, :] = r.recur_input[...]
    r.wr[1, mine, :] = r.recur_gate[...]
    r.wr[2, mine, :] = r.recur_output[...]
    for b in range(4):
        r.wr[:, b * LANE + BW : (b + 1) * LANE, :] = jnp.zeros((3, LANE - BW, D), BF16)
    r.pr[y] = jnp.zeros((PAR, LANE), F32)
    r.pr[y, 0:BW, 0:BW] = r.decay_gate[0]
    r.pr[y, BW : 2 * BW, 0:BW] = r.input_gate[0]
    r.pr[y, VEC : VEC + 4, 0:BW] = r.conv_kernel[...]
    r.pr[y, VEC + 4 : VEC + 5, 0:BW] = r.conv_bias[...]
    r.pr[y, VEC + 5 : VEC + 6, 0:BW] = r.decay_shift[...]
    r.pr[y, VEC + 6 : VEC + 7, 0:BW] = r.input_shift[...]
    r.pr[y, VEC + 7 : VEC + 8, :] = jnp.ones((1, LANE), F32)
    r.pr[y, VEC + 7 : VEC + 8, 0:BW] = r.softplus[...]
    ready()
    gather_n1 = spread_z(net, r.n1)
    half = pl.ds(pl.multiple_of(c * 512, 512), 512)
    part_p = pl.ds(pl.multiple_of(c * 104, 8), 104)
    weights_in, shared = {}, []
    for d in (1, 3, 2):
        cut = r.wr.at[0, mine, half]
        weights_in[d, 0] = net.push(cut, cut, y_peer(d))
    for d in (1, 3, 2):
        cut = r.pr.at[y, part_p, :]
        weights_in[d, 1] = net.push(cut, cut, y_peer(d))

    tail = r.n1.at[3, ROWS - 16 :, :]
    halos = [net.make(tail, r.halo, {"mp": (y * 4 + 4 + i) % 16}, "halo") for i in range(4)]

    @pl.when((z == 3) & (y < 3))
    def _():
        for halo in halos:
            halo.start()

    @pl.when(y == 0)
    def _():
        r.halo[...] = jnp.zeros((16, D), BF16)

    r.own_first[0:192, :] = r.first_gate[...]
    r.own_first[192:384, :] = r.first_value[...]
    r.own_first[384:576, :] = r.first_down[...]
    left = jnp.concatenate([r.query_proj[...], r.key_proj[...]], axis=1).astype(F32)
    right = jnp.concatenate([r.value_proj[...], r.attn_output[...]], axis=1).astype(F32)
    r.own_attn[rows_at(z * 16, 16), :] = jnp.concatenate([left, right], axis=0).astype(BF16)
    r.own_second[0:192, :] = r.second_gate[...]
    r.own_second[192:384, :] = r.second_value[...]
    r.own_second[384:576, :] = r.second_down[...]
    first_w = Gatherer(net, r.own_first, r.all_first)
    attn_w = Gatherer(net, r.own_attn, r.all_attn)
    second_w = Gatherer(net, r.own_second, r.all_second)

    def pass_on(kind):
        for d in (1, 3, 2):
            weights_in[d, kind].wait_recv()
            start = (y + 4 - d) % 4
            rows = pl.ds(pl.multiple_of(start * LANE, LANE), BW)
            if kind == 0:
                cut = r.wr.at[0, rows, half]
            elif kind == 1:
                cut = r.pr.at[start, part_p, :]
            else:
                cut = r.wr.at[1:3, rows, half]
            shared.append((kind, net.push(cut, cut, xc_peer(0, 1))))

    def arrived(kind):
        for k, copy in shared:
            if k == kind:
                copy.wait_recv()

    pass_on(0)
    for d in (1, 3, 2):
        cut = r.wr.at[1:3, mine, half]
        weights_in[d, 2] = net.push(cut, cut, y_peer(d))
    pass_on(1)
    for d in (1, 3, 2):
        gather_n1[d].wait_recv()
    r.c_all[z] = r.cot[...]
    gather_c = spread_z(net, r.c_all)
    cut = r.own_attn.at[rows_at(z * 16, 16), :]
    attn_z = [net.push(cut, cut, z_peer(d)) for d in (1, 3, 2)]
    arrived(0)
    rows_n = r.n1[...].reshape(SPAN, D)
    r.mix[8:, :] = dot_nt(rows_n, r.wr[0])

    @pl.when(y > 0)
    def _():
        halos[0].wait_recv()

    r.mix[0:8, :] = dot_nt(r.halo[...], r.wr[0])[8:, :]
    loc.store(r.n1, r.out_n1)
    loc.store(r.mix, r.out_mix)
    arrived(1)
    loc.store(r.pr, r.out_pr)
    def conv_chunk(i, _):
        first = pl.multiple_of(i * CHUNK, CHUNK)
        pos = positions(r.length, y * SPAN + first, CHUNK)
        window = r.mix[pl.ds(first, CHUNK + 8), :]
        total = lanes_of(r.pr, VEC + 4) + lanes_of(r.pr, VEC) * window[8:, :]
        for k in (1, 2, 3):
            lagged = window[8 - k : 8 - k + CHUNK, :]
            total = total + jnp.where(pos >= k, lanes_of(r.pr, VEC + k) * lagged, 0.0)
        r.conv[pl.ds(first, CHUNK), :] = total
        return 0

    lax.fori_loop(0, SPAN // CHUNK, conv_chunk, 0)
    loc.store(r.conv, r.out_conv)
    for b in range(4):
        cols = slice(b * LANE, (b + 1) * LANE)
        left = r.conv[:, b * LANE : b * LANE + BW]
        r.rate[:, cols] = low_dot(left, r.pr[b, 0:BW, :], ((1,), (0,)))
        r.opened[:, cols] = low_dot(left, r.pr[b, BW : 2 * BW, :], ((1,), (0,)))

    def gates_chunk(i, _):
        first = pl.multiple_of(i * CHUNK, CHUNK)
        rows = pl.ds(first, CHUNK)
        pos = positions(r.length, y * SPAN + first, CHUNK)
        rate = jax.nn.sigmoid(r.rate[rows, :] + lanes_of(r.pr, VEC + 5))
        opened = jax.nn.sigmoid(r.opened[rows, :] + lanes_of(r.pr, VEC + 6))
        loga = -8.0 * rate * lanes_of(r.pr, VEC + 7)
        r.rate[rows, :] = rate
        r.opened[rows, :] = opened
        r.fac[rows, :] = jnp.where(pos > 0, jnp.exp(loga), 0.0)
        r.state[pl.ds(first + 8, CHUNK), :] = (
            jnp.sqrt(neg_expm1(2.0 * loga)) * opened * r.conv[rows, :]
        )
        return 0

    lax.fori_loop(0, SPAN // CHUNK, gates_chunk, 0)
    loc.store(r.rate, r.out_rate)
    loc.store(r.opened, r.out_opened)
    row = lax.broadcasted_iota(jnp.int32, (8, CH), 0)

    def step(i, carry):
        held, prod = carry
        rows = rows_at(i * 8, 8)
        srows = rows_at(i * 8 + 8, 8)
        a = r.fac[rows, :]
        h = r.state[srows, :]
        for s in (1, 2, 4):
            h = h + a * jnp.where(row >= s, pltpu.roll(h, s, 0), 0.0)
            a = a * jnp.where(row >= s, pltpu.roll(a, s, 0), 1.0)
        h = h + a * held
        a = a * prod
        r.state[srows, :] = h
        r.acum[rows, :] = a
        return h[7:8, :], a[7:8, :]

    zero = jnp.zeros((1, CH), F32)
    last_h, last_a = lax.fori_loop(0, SPAN // 8, step, (zero, zero + 1.0), unroll=4)
    edges_in = share_edges(net, r.edges, last_a, last_h)
    pass_on(2)
    first_w.start()
    arrived(2)
    loc.store(r.wr, r.out_wr)
    r.gate[...] = dot_nt(rows_n, r.wr[1])
    loc.store(r.gate, r.out_gate)
    for copy in edges_in:
        copy.wait_recv()
    held = zero
    for b in range(3):
        held = jnp.where(b < y, r.edges[b, 0:1, :] * held + r.edges[b, 1:2, :], held)
    r.state[0:8, :] = jnp.broadcast_to(held, (8, CH))

    def gated_chunk(i, _):
        first = pl.multiple_of(i * CHUNK, CHUNK)
        rows = pl.ds(first, CHUNK)
        srows = pl.ds(first + 8, CHUNK)
        state = r.state[srows, :] + r.acum[rows, :] * held
        r.state[srows, :] = state
        r.gated[i // 2, rows_at(i % 2 * CHUNK, CHUNK), :] = (
            gelu(r.gate[rows, :]) * state
        ).astype(BF16)
        return 0

    lax.fori_loop(0, SPAN // CHUNK, gated_chunk, 0)
    loc.store(r.state, r.out_state)
    loc.store(r.gated, r.out_gated)
    back = {}
    for ds in HALVES:
        term = dot_nn(stack(r.gated, [(z + 4 - d) % 4 for d in ds]), r.wr[2])
        for i, d in enumerate(ds):
            if d:
                r.part1[d - 1] = block(term, i).astype(BF16)
                back[d] = net.push(r.part1.at[d - 1], r.recv1.at[d - 1], z_peer(4 - d))
            else:
                r.x1[...] = tokens + block(term, i)
    first_w.along()
    for copy in attn_z:
        copy.wait_recv()
    attn_w.start()
    total = r.x1[...]
    for d in (1, 3, 2):
        back[d].wait_recv()
        total = total + r.recv1[d - 1].astype(F32)
    r.x1[...] = total

    r.n2[z] = rms(total, r.gain_two[...]).astype(BF16)
    gather_n2 = spread_z(net, r.n2)
    loc.store(r.x1, r.out_x1)
    first_w.across()
    attn_w.along()
    first_w.finish()
    for copy in place_units(loc, r.all_first, r.w1):
        copy.wait()
    loc.store(r.w1, r.out_w1)
    back = {}
    for ds in HALVES:
        slots = [(z + 4 - d) % 4 for d in ds]
        for d in ds:
            if d:
                gather_n2[d].wait_recv()
        nb = stack(r.n2, slots)
        pg = dot_nt(nb, r.w1[0])
        pu = dot_nt(nb, r.w1[1])
        term = dot_nn((gelu(pg) * pu).astype(BF16), r.w1[2])
        for i, (d, s) in enumerate(zip(ds, slots)):
            r.pg[s] = block(pg, i)
            r.pu[s] = block(pu, i)
            if d:
                r.part2[d - 1] = block(term, i).astype(BF16)
                back[d] = net.push(r.part2.at[d - 1], r.recv2.at[d - 1], z_peer(4 - d))
            else:
                r.x2[...] = total + block(term, i)
        if ds == HALVES[0]:
            attn_w.across()
            second_w.start()
    loc.store(r.n2, r.out_n2)
    loc.store(r.pg, r.out_pg)
    loc.store(r.pu, r.out_pu)
    second_w.along()
    attn_w.finish()

    def split(i, _):
        a, b, e = i // 16, (i // 4) % 4, i % 4
        block = r.all_attn[a, b, e].astype(F32).reshape(4, 16, PAIR)
        rows = rows_at((b * 2 + a) * 128 + e * 32, 32)
        r.wa[0, rows, :] = block[:, 0:8, :].reshape(32, PAIR).astype(BF16)
        r.wa[1, rows, :] = block[:, 8:16, :].reshape(32, PAIR).astype(BF16)
        return 0

    lax.fori_loop(0, 32, split, 0)
    loc.store(r.wa, r.out_wa)
    total = r.x2[...]
    for d in (1, 3, 2):
        back[d].wait_recv()
        total = total + r.recv2[d - 1].astype(F32)
    r.x2[...] = total
    loc.store(r.x2, r.out_x2)

    n = rms(total, r.gain_three[...]).astype(BF16)
    r.n3[...] = n
    cosine = r.cosine[...]
    sine = r.sine[...]
    swap = lambda v: pltpu.roll(v, HD // 2, 1)
    key = dot_nn(n, r.wa[0, :, D:])
    r.kv[8, :, :HD] = (key * cosine + swap(key) * sine).astype(BF16)
    r.kv[8, :, HD:] = dot_nn(n, r.wa[1, :, :HD]).astype(BF16)
    copies = []
    for o in range(1, 9):
        copy = net.make(r.kv.at[8], r.kv.at[8 - o], row_peer(o))
        copies.append(copy)

        @pl.when(mp + o < 16)
        def _():
            copy.start()

        @pl.when(mp < o)
        def _():
            r.kv[8 - o] = jnp.zeros((ROWS, 2 * HD), BF16)

    loc.store(r.n3, r.out_n3)
    queries = dot_nn(n, r.wa[0, :, :D])
    for h in range(HEADS):
        query = queries[:, h * HD : (h + 1) * HD]
        r.q[h] = ((query * cosine + swap(query) * sine) * (1.0 / math.sqrt(HD))).astype(BF16)
    loc.store(r.q, r.out_q)
    row = lax.broadcasted_iota(jnp.int32, (ROWS, KEYS), 0)
    col = lax.broadcasted_iota(jnp.int32, (ROWS, KEYS), 1) - (KEYS - ROWS)
    base = mp * ROWS
    length = jnp.concatenate([r.length[...]] * 9, axis=1)
    allowed = (col + base >= 0) & (row >= col) & (row - col < WINDOW)
    allowed = allowed & ((row + base >= length) == (col + base >= length))
    r.bias[...] = jnp.where(allowed, 0.0, -1e30)
    second_w.across()
    for o in range(1, 9):

        @pl.when(mp >= o)
        def _():
            copies[o - 1].wait_recv()

    loc.store(r.kv, r.out_kv)
    pairs = r.kv[...].reshape(KEYS, 2 * HD)
    r.keys[...] = pairs[:, :HD]
    r.values[...] = pairs[:, HD:]
    r.score[...] = dot_nt(r.q[...].reshape(HEADS * ROWS, HD), r.keys[...])

    def softmax(i, _):
        rows, own = rows_at(i % 2 * 64, 64), rows_at(i * 64, 64)
        s = r.score[own, :] + r.bias[rows, :]
        e = jnp.exp(s - jnp.max(s, axis=-1, keepdims=True))
        p = e * (1.0 / jnp.sum(e, axis=-1, keepdims=True))
        r.pb[own, :] = p.astype(BF16)
        return 0

    lax.fori_loop(0, HEADS * 2, softmax, 0)
    mixed = dot_nn(r.pb[...], r.values[...])
    for h in range(HEADS):
        r.att[:, h * HD : (h + 1) * HD] = block(mixed, h).astype(BF16)
    loc.store(r.pb, r.out_pb)
    loc.store(r.att, r.out_att)
    total = total + dot_nn(r.att[...], r.wa[1, :, HD:])
    r.x3[...] = total
    r.n4[z] = rms(total, r.gain_four[...]).astype(BF16)
    gather_n4 = spread_z(net, r.n4)
    loc.store(r.x3, r.out_x3)
    for d in (1, 3, 2):
        gather_c[d].wait_recv()
    loc.store(r.c_all, r.out_c_all)
    second_w.finish()
    loc.stores += place_units(loc, r.all_second, r.out_w2)
    for d in (1, 3, 2):
        gather_n4[d].wait_recv()
    loc.store(r.n4, r.out_n4)
    loc.drain()
    net.drain()
    for o in range(1, 9):

        @pl.when(mp + o < 16)
        def _():
            copies[o - 1].wait_send()

    @pl.when((z == 3) & (y < 3))
    def _():
        for halo in halos:
            halo.wait_send()


BIG = ((SPAN, CH), F32)
TALL = ((SPAN + 8, CH), F32)
SAVED = {
    "n1": ((4, ROWS, D), BF16),
    "wr": ((3, CH, D), BF16),
    "pr": ((4, PAR, LANE), F32),
    "mix": TALL,
    "gate": BIG,
    "conv": BIG,
    "rate": BIG,
    "opened": BIG,
    "state": TALL,
    "gated": ((4, ROWS, CH), BF16),
    "x1": ((ROWS, D), F32),
    "w1": ((3, UNITS, D), BF16),
    "n2": ((4, ROWS, D), BF16),
    "pg": ((4, ROWS, UNITS), F32),
    "pu": ((4, ROWS, UNITS), F32),
    "x2": ((ROWS, D), F32),
    "wa": ((2, D, PAIR), BF16),
    "n3": ((ROWS, D), BF16),
    "q": ((HEADS, ROWS, HD), BF16),
    "kv": ((9, ROWS, 2 * HD), BF16),
    "pb": ((HEADS * ROWS, KEYS), BF16),
    "att": ((ROWS, D), BF16),
    "x3": ((ROWS, D), F32),
    "n4": ((4, ROWS, D), BF16),
    "c_all": ((4, ROWS, D), BF16),
}
BLOCKS = ((2, 4, 4, 576, LANE), BF16)


def forward(inputs):
    outs = [("out_" + k, *v, "far") for k, v in SAVED.items()]
    outs += [("out_w2", (3, UNITS, D), BF16, "far")]
    scratch = [(k, vm(*v)) for k, v in SAVED.items()]
    scratch += [
        ("fac", vm(*BIG)),
        ("acum", vm(*BIG)),
        ("edges", vm((4, 8, CH), F32)),
        ("part1", vm((3, ROWS, D), BF16)),
        ("recv1", vm((3, ROWS, D), BF16)),
        ("part2", vm((3, ROWS, D), BF16)),
        ("recv2", vm((3, ROWS, D), BF16)),
        ("own_first", vm((576, LANE), BF16)),
        ("own_second", vm((576, LANE), BF16)),
        ("own_attn", vm((64, PAIR), BF16)),
        ("all_first", vm(*BLOCKS)),
        ("all_second", vm(*BLOCKS)),
        ("all_attn", vm((2, 4, 4, 64, PAIR), BF16)),
        ("halo", vm((16, D), BF16)),
        ("bias", vm((ROWS, KEYS), F32)),
        ("score", vm((HEADS * ROWS, KEYS), F32)),
        ("keys", vm((KEYS, HD), BF16)),
        ("values", vm((KEYS, HD), BF16)),
        ("send", dma(100)),
        ("recv", dma(100)),
        ("sems", dma(230)),
    ]
    return run(
        forward_body, [(k, v, "near") for k, v in inputs.items()], outs, scratch, 1, 10**10
    )


def middle_body(r):
    _, _, _, z = place()
    mp = lax.axis_index("mp")
    ready = greet(all_peers(True))
    net, loc = Net(r.send, r.recv), Local(r.sems)
    loads = {
        k: loc.load(getattr(r, "far_" + k), getattr(r, k))
        for k in ("w2", "n4", "c_all", "wa", "kv", "pb", "q", "att", "n3", "x2")
    }
    x = r.x3[...]
    c = r.cot[...].astype(F32)
    for k in ("w2", "n4", "c_all"):
        loads[k].wait()
    back_d, back_o = {}, {}
    for ds in HALVES:
        slots = [(z + 4 - d) % 4 for d in ds]
        nb = stack(r.n4, slots)
        pg = dot_nt(nb, r.w2[0])
        pu = dot_nt(nb, r.w2[1])
        act, slope = gelu_both(pg)
        hid = (act * pu).astype(BF16)
        dh = dot_nt(stack(r.c_all, slots), r.w2[2])
        dpg = (dh * pu * slope).astype(BF16)
        dpu = (dh * act).astype(BF16)
        term = dot_nn(dpg, r.w2[0]) + dot_nn(dpu, r.w2[1])
        if ds == HALVES[0]:
            ready()
        for i, (d, s) in enumerate(zip(ds, slots)):
            r.hid[s] = block(hid, i)
            r.dpg[s] = block(dpg, i)
            r.dpu[s] = block(dpu, i)
            if d == 0:
                r.own_d[...] = block(term, i)
            else:
                r.part_d[d - 1] = block(term, i).astype(BF16)
                back_d[d] = net.push(r.part_d.at[d - 1], r.recv_d.at[d - 1], z_peer(4 - d))
    unit_grads(((r.dpg, r.n4), (r.dpu, r.n4), (r.hid, r.c_all)), r.gw2)
    reducer = Reducer(net, r.gw2, r, "red")
    reducer.start()
    dn = r.own_d[...]
    for d in (1, 3, 2):
        back_d[d].wait_recv()
        dn = dn + r.recv_d[d - 1].astype(F32)
    dv, r.gg_four[...] = rms_back(dn, x, r.gain_four[...])
    c = c + dv

    for ds in HALVES:
        slots = [(z + 4 - d) % 4 for d in ds]
        term = dot_nn(stack(r.hid, slots), r.w2[2])
        for i, d in enumerate(ds):
            if d == 0:
                r.outputs[...] = x + block(term, i)
            else:
                r.part_o[d - 1] = block(term, i).astype(BF16)
                back_o[d] = net.push(r.part_o.at[d - 1], r.recv_o.at[d - 1], z_peer(4 - d))

    for k in ("wa", "kv", "pb", "q", "att", "n3", "x2"):
        loads[k].wait()
    cb = c.astype(BF16)
    datt = dot_nt(cb, r.wa[1, :, HD:]).astype(BF16)
    for h in range(HEADS):
        r.datt[h] = datt[:, h * HD : (h + 1) * HD]
    cosine = r.cosine[...]
    sine = r.sine[...]
    swap = lambda v: pltpu.roll(v, HD // 2, 1)
    pairs = r.kv[...].reshape(KEYS, 2 * HD)
    r.keys[...] = pairs[:, :HD]
    r.values[...] = pairs[:, HD:]
    datts = r.datt[...].reshape(HEADS * ROWS, HD)
    r.score[...] = dot_nt(datts, r.values[...])

    def scores(i, _):
        own = rows_at(i * 64, 64)
        dp = r.score[own, :]
        p = r.pb[own, :].astype(F32)
        ds = p * (dp - jnp.sum(p * dp, axis=-1, keepdims=True))
        r.ds[own, :] = ds.astype(BF16)
        return 0

    lax.fori_loop(0, HEADS * 2, scores, 0)
    dqs = dot_nn(r.ds[...], r.keys[...])
    for h in range(HEADS):
        dq = block(dqs, h) * (1.0 / math.sqrt(HD))
        r.dqkv[:, h * HD : (h + 1) * HD] = (dq * cosine - swap(dq) * sine).astype(BF16)
    r.turned[0] = dot_tn(r.q[...].reshape(HEADS * ROWS, HD), r.ds[...])
    r.turned[1] = dot_tn(datts, r.pb[...])
    copies = {}
    for o in (1, 2, 3, 4, 5, 6, 7, 8):
        keys = slice((8 - o) * ROWS, (9 - o) * ROWS)
        r.part_kv[o - 1, :, :HD] = r.turned[0, :, keys].T.astype(BF16)
        r.part_kv[o - 1, :, HD:] = r.turned[1, :, keys].T.astype(BF16)
        copy = net.make(r.part_kv.at[o - 1], r.recv_kv.at[o - 1], row_peer(-o))
        copies[o] = copy

        @pl.when(mp >= o)
        def _():
            copy.start()

        @pl.when(mp + o >= 16)
        def _():
            r.recv_kv[o - 1] = jnp.zeros((ROWS, 2 * HD), BF16)

    dn = dot_nt(r.dqkv[...], r.wa[0, :, :D])
    own_k = r.turned[0, :, KEYS - ROWS :].T
    own_v = r.turned[1, :, KEYS - ROWS :].T
    reducer.along_one()
    for o in range(1, 9):

        @pl.when(mp + o < 16)
        def _():
            copies[o].wait_recv()

        own_k = own_k + r.recv_kv[o - 1, :, :HD].astype(F32)
        own_v = own_v + r.recv_kv[o - 1, :, HD:].astype(F32)
    dk = (own_k * cosine - swap(own_k) * sine).astype(BF16)
    dv = own_v.astype(BF16)
    dn = dn + dot_nt(dk, r.wa[0, :, D:]) + dot_nt(dv, r.wa[1, :, :HD])
    back, r.gg_three[...] = rms_back(dn, r.x2[...], r.gain_three[...])
    c = c + back
    r.c2[...] = c
    r.c2_all[z] = c.astype(BF16)
    gather_c = spread_z(net, r.c2_all)
    n = r.n3[...].T
    att = r.att[...].T

    for t in range(4):
        cols = slice(t * 256, (t + 1) * 256)
        r.right[:, HD + t * 256 : HD + (t + 1) * 256] = dot_nn(att, cb[:, cols])
        r.score[:, cols] = dot_nn(n, r.dqkv[:, cols])
    r.score[:, D:] = dot_nn(n, dk)
    r.right[:, :HD] = dot_nn(n, dv)
    reducer.along_two()

    def lower(i, _):
        a, e, b = i // 8, i // 4 % 2, i % 4
        rows = rows_at(i * 32, 32)
        left = r.score[rows, :].reshape(4, 8, PAIR)
        right = r.right[rows, :].reshape(4, 8, PAIR)
        both = jnp.concatenate([left, right], axis=1)
        r.gw_attn[e, a, b] = both.reshape(64, PAIR).astype(BF16)
        return 0

    lax.fori_loop(0, 32, lower, 0)
    loc.store(r.gw_attn, r.out_gw_attn)
    total = r.outputs[...]
    for d in (1, 3, 2):
        back_o[d].wait_recv()
        total = total + r.recv_o[d - 1].astype(F32)
    r.outputs[...] = total
    for d in (1, 3, 2):
        gather_c[d].wait_recv()
    loc.store(r.c2_all, r.out_c2_all)
    a, b = reducer.finish()
    r.second_out[0:288, :] = a
    r.second_out[288:, :] = b
    loc.drain()
    net.drain()
    for o in range(1, 9):

        @pl.when(mp >= o)
        def _():
            copies[o].wait_send()


def middle(near, far):
    ins = [(k, v, "near") for k, v in near.items()]
    ins += [("far_" + k, v, "far") for k, v in far.items()]
    outs = [
        ("outputs", (ROWS, D), F32, "near"),
        ("c2", (ROWS, D), F32, "near"),
        ("gg_four", (1, D), F32, "near"),
        ("gg_three", (1, D), F32, "near"),
        ("second_out", (576, LANE), F32, "near"),
        ("out_gw_attn", (2, 4, 4, 64, PAIR), BF16, "far"),
        ("out_c2_all", (4, ROWS, D), BF16, "far"),
    ]
    units = ((4, ROWS, UNITS), BF16)
    third = ((3, ROWS, D), BF16)
    scratch = [(k, vm(*SAVED[k])) for k in far if k in SAVED]
    scratch += [
        ("w2", vm((3, UNITS, D), BF16)),
        ("c2_all", vm((4, ROWS, D), BF16)),
        ("score", vm((HEADS * ROWS, KEYS), F32)),
        ("keys", vm((KEYS, HD), BF16)),
        ("values", vm((KEYS, HD), BF16)),
        ("turned", vm((2, HD, KEYS), F32)),
        ("hid", vm(*units)),
        ("dpg", vm(*units)),
        ("dpu", vm(*units)),
        ("own_d", vm((ROWS, D), F32)),
        ("part_d", vm(*third)),
        ("recv_d", vm(*third)),
        ("part_o", vm(*third)),
        ("recv_o", vm(*third)),
        ("gw2", vm(*BLOCKS)),
        ("datt", vm((HEADS, ROWS, HD), BF16)),
        ("ds", vm((HEADS * ROWS, KEYS), BF16)),
        ("part_kv", vm((8, ROWS, 2 * HD), BF16)),
        ("recv_kv", vm((8, ROWS, 2 * HD), BF16)),
        ("dqkv", vm((ROWS, D), BF16)),
        ("right", vm((D, PAIR), F32)),
        ("gw_attn", vm((2, 4, 4, 64, PAIR), BF16)),
        *Reducer.scratch("red", 576, LANE),
        ("send", dma(40)),
        ("recv", dma(40)),
        ("sems", dma(16)),
    ]
    return run(middle_body, ins, outs, scratch, 2, 10**10)


def last_body(r):
    x, c, y, z = place()
    dp = lax.axis_index("dp")
    ready = greet(all_peers(False) + [xc_peer(d, 1) for d in (1, 2, 3)])
    net, loc = Net(r.send, r.recv), Local(r.sems)
    attn_in = loc.load(r.far_gw_attn, r.gw_attn)
    loads = {
        k: loc.load(getattr(r, "far_" + k), getattr(r, k))
        for k in ("w1", "pg", "pu", "c2_all", "n2", "wr", "gate", "state", "rate", "pr", "opened", "conv",
                  "mix", "n1", "gated")
    }
    need = lambda *names: [loads[k].wait() for k in names]
    upstream = r.c2[...]
    need("w1", "pg", "pu", "c2_all")
    red_attn = Reducer(net, r.gw_attn, r, "rat")
    back = {}
    for ds in HALVES:
        slots = [(z + 4 - d) % 4 for d in ds]
        pg = stack(r.pg, slots)
        pu = stack(r.pu, slots)
        act, slope = gelu_both(pg)
        hid = (act * pu).astype(BF16)
        dh = dot_nt(stack(r.c2_all, slots), r.w1[2])
        dpg = (dh * pu * slope).astype(BF16)
        dpu = (dh * act).astype(BF16)
        term = dot_nn(dpg, r.w1[0]) + dot_nn(dpu, r.w1[1])
        if ds == HALVES[0]:
            ready()
        for i, (d, s) in enumerate(zip(ds, slots)):
            r.hid[s] = block(hid, i)
            r.dpg[s] = block(dpg, i)
            r.dpu[s] = block(dpu, i)
            if d == 0:
                r.grad_tokens[...] = block(term, i)
            else:
                r.part1[d - 1] = block(term, i).astype(BF16)
                back[d] = net.push(r.part1.at[d - 1], r.recv1.at[d - 1], z_peer(4 - d))
        if ds == HALVES[0]:
            attn_in.wait()
            red_attn.start()
    red_attn.along_one()
    need("n2")
    unit_grads(((r.dpg, r.n2), (r.dpu, r.n2), (r.hid, r.c2_all)), r.gw1)
    red_first = Reducer(net, r.gw1, r, "rff")
    red_first.start()
    red_attn.along_two()
    dn = r.grad_tokens[...]
    for d in (1, 3, 2):
        back[d].wait_recv()
        dn = dn + r.recv1[d - 1].astype(F32)
    dv, gg_two = rms_back(dn, r.x1[...], r.gain_two[...])
    upstream = upstream + dv
    r.c1[...] = upstream

    r.c1_all[z] = upstream.astype(BF16)
    gather_c = spread_z(net, r.c1_all)
    a, b = red_attn.finish()
    r.z_out[0:2] = a.astype(BF16).reshape(2, 16, PAIR)
    r.z_out[2:4] = b.astype(BF16).reshape(2, 16, PAIR)
    z_in = [
        net.push(r.z_out.at[(z + d) % 4], r.z_in.at[d - 1], z_peer(d)) for d in (1, 3, 2)
    ]
    need("wr")
    for ds in STEPS:
        slots = [(z + 4 - d) % 4 for d in ds]
        for d in ds:
            if d:
                gather_c[d].wait_recv()
        term = dot_nt(stack(r.c1_all, slots), r.wr[2])
        for i, (d, s) in enumerate(zip(ds, slots)):
            r.du[rows_at(s * ROWS, ROWS), :] = block(term, i)
            if d == 0:
                red_first.along_one()
    need("gate", "state", "rate", "pr")

    def decay_of(rows, first):
        pos = positions(r.length, y * SPAN + first, CHUNK)
        loga = -8.0 * r.rate[rows, :] * lanes_of(r.pr, VEC + 7)
        return loga, jnp.exp(loga), pos

    def first_chunk(i, _):
        first = pl.multiple_of(i * CHUNK, CHUNK)
        rows = pl.ds(first, CHUNK)
        act, slope = gelu_both(r.gate[rows, :])
        dgated = r.du[rows, :]
        dgate = dgated * r.state[pl.ds(first + 8, CHUNK), :] * slope
        r.hid[i // 2, rows_at(i % 2 * CHUNK, CHUNK), 0:CH] = dgate.astype(BF16)
        r.du[rows, :] = dgated * act
        _, decay, pos = decay_of(rows, first)
        r.fac[rows, :] = jnp.where(pos > 0, decay, 0.0)
        return 0

    lax.fori_loop(0, SPAN // CHUNK, first_chunk, 0)
    row = lax.broadcasted_iota(jnp.int32, (8, CH), 0)

    def step(i, carry):
        held, prod = carry
        rows = rows_at((SPAN // 8 - 1 - i) * 8, 8)
        m = r.fac[rows, :]
        u = r.du[rows, :]
        e = m * u
        for s in (1, 2, 4):
            inside = row < 8 - s
            e = e + m * jnp.where(inside, pltpu.roll(e, 8 - s, 0), 0.0)
            m = m * jnp.where(inside, pltpu.roll(m, 8 - s, 0), 1.0)
        e = e + m * held
        m = m * prod
        r.du[rows, :] = u + jnp.where(row < 7, pltpu.roll(e, 7, 0), held)
        r.acum[rows, :] = jnp.where(row < 7, pltpu.roll(m, 7, 0), prod)
        return e[0:1, :], m[0:1, :]

    zero = jnp.zeros((1, CH), F32)
    first_e, first_m = lax.fori_loop(0, SPAN // 8, step, (zero, zero + 1.0), unroll=4)
    edges_in = share_edges(net, r.edges, first_m, first_e)
    need("opened", "conv", "mix", "n1", "gated")

    def output_grads(out, w, left, right):
        for half in range(2):
            cut = left[:, :, half * 256 : half * 256 + 256].reshape(SPAN, 256)
            grad = dot_tn(cut, right[...].reshape(SPAN, D))
            for j in range(2):
                for part in range(8):
                    out[part % 2, part // 2, half * 2 + j, w * BW : (w + 1) * BW, :] = grad[
                        j * LANE : j * LANE + BW, part * LANE : (part + 1) * LANE
                    ].astype(BF16)

    output_grads(r.gwa, 0, r.hid, r.n1)
    output_grads(r.gwa, 1, r.gated, r.c1_all)
    red_a = Reducer(net, r.gwa, r, "rea")
    red_a.start()
    for copy in edges_in:
        copy.wait_recv()
    held = zero
    for b in (3, 2, 1):
        held = jnp.where(b > y, r.edges[b, 0:1, :] * held + r.edges[b, 1:2, :], held)

    def second_chunk(i, dsp):
        first = pl.multiple_of(i * CHUNK, CHUNK)
        rows = pl.ds(first, CHUNK)
        ds = r.du[rows, :] + r.acum[rows, :] * held
        loga, decay, pos = decay_of(rows, first)
        rate = r.rate[rows, :]
        opened = r.opened[rows, :]
        conv = r.conv[rows, :]
        before = r.state[pl.ds(first, CHUNK + 8), :][7 : 7 + CHUNK, :]
        beta = jnp.sqrt(neg_expm1(2.0 * loga))
        dloga = jnp.where(pos > 0, ds * before * decay, 0.0)
        dloga = dloga - ds * opened * conv * (decay * decay) / beta
        dopened = ds * beta * conv
        r.du[rows, :] = ds * beta * opened
        r.acum[rows, :] = dloga * (-8.0 * lanes_of(r.pr, VEC + 7)) * rate * (1.0 - rate)
        r.fac[rows, :] = dopened * opened * (1.0 - opened)
        return dsp + jnp.sum(dloga * (-8.0 * rate), axis=0, keepdims=True)

    dsp = lax.fori_loop(0, SPAN // CHUNK, second_chunk, zero)
    for b in range(4):
        cols = slice(b * LANE, (b + 1) * LANE)
        r.du[0:SPAN, cols] = (
            r.du[0:SPAN, cols]
            + jnp.pad(
                low_dot(r.acum[:, cols], r.pr[b, 0:BW, :], ((1,), (1,)))
                + low_dot(r.fac[:, cols], r.pr[b, BW : 2 * BW, :], ((1,), (1,))),
                ((0, 0), (0, LANE - BW)),
            )
        )
    halo = net.make(r.du.at[0:8], r.du.at[SPAN : SPAN + 8], y_peer(3))

    @pl.when(y > 0)
    def _():
        halo.start()

    @pl.when(y == 3)
    def _():
        r.du[SPAN : SPAN + 8, :] = jnp.zeros((8, CH), F32)

    red_first.along_two()
    for b in range(4):
        cols = slice(b * LANE, (b + 1) * LANE)
        left = r.conv[:, b * LANE : b * LANE + BW]
        r.gp[b, 0:BW, :] = low_dot(left, r.acum[:, cols], ((0,), (0,)))
        r.gp[b, BW : 2 * BW, :] = low_dot(left, r.fac[:, cols], ((0,), (0,)))
    red_a.along_one()

    @pl.when(y < 3)
    def _():
        halo.wait_recv()

    def third_chunk(i, sums):
        first = pl.multiple_of(i * CHUNK, CHUNK)
        rows = pl.ds(first, CHUNK)
        pos = positions(r.length, y * SPAN + first, CHUNK + 8)
        dwin = r.du[pl.ds(first, CHUNK + 8), :]
        mwin = r.mix[pl.ds(first, CHUNK + 8), :]
        dconv = dwin[:CHUNK, :]
        total = lanes_of(r.pr, VEC) * dconv
        taps = [jnp.sum(dconv * mwin[8:, :], axis=0, keepdims=True)]
        for k in (1, 2, 3):
            masked = jnp.where(pos >= k, dwin, 0.0)
            total = total + lanes_of(r.pr, VEC + k) * masked[k : k + CHUNK, :]
            taps.append(
                jnp.sum(masked[:CHUNK, :] * mwin[8 - k : 8 - k + CHUNK, :], axis=0, keepdims=True)
            )
        r.dpg[i // 2, rows_at(i % 2 * CHUNK, CHUNK), 0:CH] = total.astype(BF16)
        taps.append(jnp.sum(dconv, axis=0, keepdims=True))
        taps.append(jnp.sum(r.acum[rows, :], axis=0, keepdims=True))
        taps.append(jnp.sum(r.fac[rows, :], axis=0, keepdims=True))
        return tuple(a + b for a, b in zip(sums, taps))

    sums = lax.fori_loop(0, SPAN // CHUNK, third_chunk, (zero,) * 7)
    back = {}
    for ds in HALVES:
        slots = [(z + 4 - d) % 4 for d in ds]
        mixes = stack(r.dpg, slots)[:, 0:CH]
        gates = stack(r.hid, slots)[:, 0:CH]
        term = dot_nn(mixes, r.wr[0]) + dot_nn(gates, r.wr[1])
        for i, d in enumerate(ds):
            if d:
                r.part2[d - 1] = block(term, i).astype(BF16)
                back[d] = net.push(r.part2.at[d - 1], r.recv2.at[d - 1], z_peer(4 - d))
            else:
                r.grad_tokens[...] = block(term, i)
    output_grads(r.gwb, 0, r.dpg, r.n1)
    for b in range(4):
        cols = slice(b * LANE, (b + 1) * LANE)
        for k, row_sum in enumerate(sums + (dsp,)):
            r.gp[b, VEC + k : VEC + k + 1, :] = row_sum[:, cols]
        r.gp[b, 200:, :] = jnp.zeros((56, LANE), F32)
        for part in range(8):
            r.gwb[part % 2, part // 2, b, BW:, :] = r.gp[
                b, part * 32 : part * 32 + 32, :
            ].astype(BF16)
    red_b = Reducer(net, r.gwb, r, "reb")
    red_b.start()
    red_a.along_two()

    def spread(stage, first, peers):
        r.gain_out[stage] = r.gains[...]
        return [
            net.push(r.gain_out.at[stage], r.gain_in.at[first + i], peer)
            for i, peer in enumerate(peers)
        ]

    def collect(first, mine):
        total = r.gains[...]
        for i, copy in enumerate(mine):
            copy.wait_recv()
            total = total + r.gain_in[first + i]
        r.gains[...] = total

    def share(reducer, whole):
        a, b = reducer.finish()
        half = reducer.half
        whole[dp, 0:half, :] = a.astype(BF16)
        whole[dp, half:, :] = b.astype(BF16)
        cut = whole.at[dp]
        return [
            net.push(cut, cut, xc_peer(dx, dc))
            for dx, dc in ((1, 0), (3, 0), (2, 0), (1, 1), (3, 1), (2, 1), (0, 1))
        ]

    red_b.along_one()
    dn = r.grad_tokens[...]
    for d in (1, 3, 2):
        back[d].wait_recv()
        dn = dn + r.recv2[d - 1].astype(F32)
    dv, gg_one = rms_back(dn, r.tok[...].astype(F32), r.gain_one[...])
    r.grad_tokens[...] = r.c1[...] + dv
    r.gains[...] = jnp.concatenate(
        [gg_one, gg_two, r.gg_three[...], r.gg_four[...], jnp.zeros((4, D), F32)], axis=0
    )
    mine = spread(0, 0, [xc_peer(0, 1)])
    shares = share(red_a, r.recur_a)
    collect(0, mine)
    mine = spread(1, 1, [xc_peer(d, 0) for d in (1, 3, 2)])
    red_b.along_two()
    a, b = red_first.finish()
    r.first_out[0:288, :] = a
    r.first_out[288:, :] = b
    collect(1, mine)
    mine = spread(2, 4, [y_peer(d) for d in (1, 3, 2)])
    shares += share(red_b, r.recur_b)
    total = r.z_out[z].astype(F32)
    for copy in z_in:
        copy.wait_recv()
    for d in range(3):
        total = total + r.z_in[d].astype(F32)
    r.attn_out[...] = total
    collect(4, mine)
    mine = spread(3, 7, [z_peer(d) for d in (1, 3, 2)])
    collect(7, mine)
    for copy in shares:
        copy.wait_recv()
    net.drain()

    @pl.when(y > 0)
    def _():
        halo.wait_send()


def last(near, far):
    ins = [(k, v, "near") for k, v in near.items()]
    ins += [("far_" + k, v, "far") for k, v in far.items()]
    outs = [
        ("grad_tokens", (ROWS, D), F32, "near"),
        ("gains", (8, D), F32, "near"),
        ("first_out", (576, LANE), F32, "near"),
        ("attn_out", (16, PAIR), F32, "near"),
        ("recur_a", (8, 192, LANE), BF16, "near"),
        ("recur_b", (8, 128, LANE), BF16, "near"),
    ]
    units = ((4, ROWS, UNITS), BF16)
    third = ((3, ROWS, D), BF16)
    whole = ((4, ROWS, D), BF16)
    scratch = [(k, vm(*SAVED[k])) for k in far if k in SAVED]
    scratch += [
        ("gw_attn", vm((2, 4, 4, 64, PAIR), BF16)),
        ("c2_all", vm(*whole)),
        ("c1_all", vm(*whole)),
        ("c1", vm((ROWS, D), F32)),
        ("hid", vm(*units)),
        ("dpg", vm(*units)),
        ("dpu", vm(*units)),
        ("part1", vm(*third)),
        ("recv1", vm(*third)),
        ("part2", vm(*third)),
        ("recv2", vm(*third)),
        ("gw1", vm(*BLOCKS)),
        ("z_out", vm((4, 16, PAIR), BF16)),
        ("z_in", vm((3, 16, PAIR), BF16)),
        ("du", vm(*TALL)),
        ("fac", vm(*BIG)),
        ("acum", vm(*BIG)),
        ("edges", vm((4, 8, CH), F32)),
        ("gp", vm((4, 256, LANE), F32)),
        ("gwa", vm((2, 4, 4, 192, LANE), BF16)),
        ("gwb", vm((2, 4, 4, 128, LANE), BF16)),
        ("gain_in", vm((10, 8, D), F32)),
        ("gain_out", vm((4, 8, D), F32)),
        *Reducer.scratch("rat", 64, PAIR),
        *Reducer.scratch("rff", 576, LANE),
        *Reducer.scratch("rea", 192, LANE),
        *Reducer.scratch("reb", 128, LANE),
        ("send", dma(96)),
        ("recv", dma(96)),
        ("sems", dma(17)),
    ]
    return run(last_body, ins, outs, scratch, 3, 10**10)


def output_body(r):
    r.outputs[...] = r.in_outputs[...]
    r.tokens[...] = r.in_tokens[...]
    for i, name in enumerate(("norm_one", "norm_two", "norm_three", "norm_four")):
        getattr(r, name)[...] = r.gains[i : i + 1, :]
    for part in range(8):
        rows = slice(part * LANE, (part + 1) * LANE)
        r.recur_gate[:, rows] = r.recur_a[part, 0:BW, :].astype(F32)
        r.recur_output[:, rows] = r.recur_a[part, BW:, :].astype(F32)
        r.recur_input[:, rows] = r.recur_b[part, 0:BW, :].astype(F32)
    params = r.recur_b[:, BW:, :].astype(F32).reshape(256, LANE)
    r.decay_gate[0] = params[0:BW, :BW]
    r.input_gate[0] = params[BW : 2 * BW, :BW]
    r.conv_kernel[...] = params[VEC : VEC + 4, :BW]
    r.conv_bias[...] = params[VEC + 4 : VEC + 5, :BW]
    r.decay_shift[...] = params[VEC + 5 : VEC + 6, :BW]
    r.input_shift[...] = params[VEC + 6 : VEC + 7, :BW]
    r.decay_param[...] = params[VEC + 7 : VEC + 8, :BW] * r.slope[...]
    for name in ("first", "second"):
        summed = getattr(r, name)
        getattr(r, name + "_gate")[...] = summed[0:192, :]
        getattr(r, name + "_value")[...] = summed[192:384, :]
        getattr(r, name + "_down")[...] = summed[384:, :]
    r.query_proj[...] = r.attn[0:8, :D]
    r.key_proj[...] = r.attn[0:8, D:]
    r.value_proj[...] = r.attn[8:16, :HD]
    r.attn_output[...] = r.attn[8:16, HD:]


OUTPUTS = (
    ("outputs", (ROWS, D)), ("tokens", (ROWS, D)), ("norm_one", (1, D)),
    ("recur_input", (BW, D)), ("recur_gate", (BW, D)), ("conv_kernel", (4, BW)),
    ("conv_bias", (1, BW)), ("decay_gate", (1, BW, BW)), ("decay_shift", (1, BW)),
    ("input_gate", (1, BW, BW)), ("input_shift", (1, BW)), ("decay_param", (1, BW)),
    ("recur_output", (BW, D)), ("norm_two", (1, D)), ("first_gate", (192, 128)),
    ("first_value", (192, 128)), ("first_down", (192, 128)), ("norm_three", (1, D)),
    ("query_proj", (8, D)), ("key_proj", (8, HD)), ("value_proj", (8, HD)),
    ("attn_output", (8, D)), ("norm_four", (1, D)), ("second_gate", (192, 128)),
    ("second_value", (192, 128)), ("second_down", (192, 128)),
)
FLAT = (
    "norm_one", "conv_bias", "decay_shift", "input_shift", "decay_param", "norm_two",
    "norm_three", "norm_four",
)
TURNED = (
    "recur_input", "recur_gate", "first_gate", "first_value", "second_gate", "second_value",
)


def local(
    tokens, lengths, cotangent, norm_one, recur_input, recur_gate, conv_kernel, conv_bias,
    decay_gate, decay_shift, input_gate, input_shift, decay_param, recur_output, norm_two,
    first_gate, first_value, first_down, norm_three, query_proj, key_proj, value_proj,
    attn_output, norm_four, second_gate, second_value, second_down,
):
    length = jnp.broadcast_to(lengths.reshape(1, 1), (1, LANE))
    gain_one, gain_two, gain_three, gain_four = (
        g.reshape(1, D) for g in (norm_one, norm_two, norm_three, norm_four)
    )
    flat = lambda v: v.reshape(1, BW)

    index = lax.axis_index("mp") * ROWS + jnp.arange(ROWS, dtype=jnp.int32)
    position = jnp.where(index >= lengths[0], index - lengths[0], index)
    frequency = 10000.0 ** (-2.0 * jnp.arange(HD // 2, dtype=F32) / HD)
    angle = position.astype(F32)[:, None] * frequency[None, :]
    cosine = jnp.concatenate([jnp.cos(angle)] * 2, axis=1)
    sine = jnp.concatenate([-jnp.sin(angle), jnp.sin(angle)], axis=1)

    saved = forward(
        dict(
            tok=tokens, cot=cotangent, length=length, cosine=cosine, sine=sine,
            gain_one=gain_one, gain_two=gain_two, gain_three=gain_three,
            gain_four=gain_four, recur_input=recur_input.T, recur_gate=recur_gate.T, recur_output=recur_output,
            conv_kernel=conv_kernel, conv_bias=flat(conv_bias), decay_gate=decay_gate,
            decay_shift=flat(decay_shift), input_gate=input_gate,
            input_shift=flat(input_shift), softplus=flat(jax.nn.softplus(-decay_param)),
            first_gate=first_gate.T, first_value=first_value.T, first_down=first_down,
            query_proj=query_proj, key_proj=key_proj, value_proj=value_proj,
            attn_output=attn_output, second_gate=second_gate.T, second_value=second_value.T,
            second_down=second_down,
        )
    )
    kept = lambda *names: {k: saved["out_" + k] for k in names}
    mid = middle(
        dict(
            x3=saved["out_x3"], cot=cotangent, gain_four=gain_four, gain_three=gain_three,
            cosine=cosine, sine=sine,
        ),
        kept("w2", "n4", "c_all", "wa", "kv", "pb", "q", "att", "n3", "x2"),
    )
    end = last(
        dict(
            c2=mid["c2"], x1=saved["out_x1"], tok=tokens, length=length, gain_one=gain_one,
            gain_two=gain_two, gg_three=mid["gg_three"], gg_four=mid["gg_four"],
        ),
        dict(
            kept(
                "w1", "pg", "pu", "n2", "wr", "gate", "state", "rate", "pr", "opened", "conv",
                "mix", "n1", "gated",
            ),
            gw_attn=mid["out_gw_attn"],
            c2_all=mid["out_c2_all"],
        ),
    )
    results = run(
        output_body,
        [
            ("in_outputs", mid["outputs"], "near"),
            ("in_tokens", end["grad_tokens"], "near"),
            ("gains", end["gains"], "near"),
            ("recur_a", end["recur_a"], "near"),
            ("recur_b", end["recur_b"], "near"),
            ("first", end["first_out"], "near"),
            ("second", mid["second_out"], "near"),
            ("attn", end["attn_out"], "near"),
            ("slope", flat(-jax.nn.sigmoid(-decay_param)), "near"),
        ],
        [(name, shape, F32, "near") for name, shape in OUTPUTS],
        [],
    )
    for name in FLAT:
        results[name] = results[name].reshape(-1)
    for name in TURNED:
        results[name] = results[name].T
    return tuple(results[name] for name, _ in OUTPUTS)


def solution(mesh):
    rows = P(("dp", "mp"), None)
    cols = P(None, "mp")
    one = P("mp")
    blocks = P("mp", None, None)
    tile = P("dp", "mp")
    weights = (
        P(), cols, cols, cols, one, blocks, one, blocks, one, one, P("mp", None),
        P(), tile, tile, P("mp", "dp"),
        P(), rows, rows, rows, rows,
        P(), tile, tile, P("mp", "dp"),
    )
    return jax.shard_map(
        local,
        mesh=mesh,
        in_specs=(rows, P("dp"), rows, *weights),
        out_specs=(rows, rows, *weights),
        check_vma=False,
    )
```

profile of v0, /device:TPU:0, one launch (start us, length us, event | category | flops | bytes accessed | tf_op | source)
XLA Modules:
  0.0 276.4 jit_solution(5353223831109677007)
XLA Ops:
  1.3 0.5 broadcast_in_dim.10.refs_2_.refs_3_
  1.9 1.2 negate_bitcast_fusion
  3.1 0.3 fusion
  3.4 0.8 pad_maximum_fusion
  4.1 106.5 %shard_map.458 = (bf16[4,128,1024]{2,1,0:T(8,128)(2,1)}, bf16[3,512,1024]{2,1,0:T(8,128)(2,1)}, f32[4,208,128]{2,1,0:T(8,128)}, f32[520,512]{1,0:T(8,128)}, f32[...) custom-call(bf16[128,1024]{1,0:T(8,128)(2,1)} %refs_2_.1, ...), custom_call_target="tpu_custom_call" | custom-call | flops 10000000000 | bytes 16777216 | tf_op jit(solution)/shard_map/pallas_call | solution.py:130
  110.7 67.2 %shard_map.459 = (f32[128,1024]{1,0:T(8,128)}, f32[128,1024]{1,0:T(8,128)}, f32[1,1024]{1,0:T(1,128)}, f32[1,1024]{1,0:T(1,128)}, f32[576,128]{1,0:T(8,128)}, /*...) custom-call(f32[128,1024]{1,0:T(8,128)} %get-tuple-element.91.refs_0_, bf16[128,1024]{1,0:T(8,128)(2,1)} %refs_1_.3, ...), custom_call_target="tpu_custom_call" | custom-call | flops 10000000000 | bytes 16777216 | tf_op jit(solution)/shard_map/pallas_call | solution.py:130
  177.8 95.0 %shard_map.460 = (f32[128,1024]{1,0:T(8,128)}, f32[8,1024]{1,0:T(8,128)}, f32[576,128]{1,0:T(8,128)}, f32[16,1152]{1,0:T(8,128)}, bf16[8,192,128]{2,1,0:T(8,128)(2,1)}, /*index=5*/bf16[8,128,128]{2,1,0:T(8,128)(2,1)}) custom-call(f32[128,1024]{1,0:T(8,128)} %get-tuple-element.103.refs_0_, f32[128,1024]{1,0:T(8,128)} %get-tuple-element.104.refs_1_, ...), custom_call_target="tpu_custom_call" | custom-call | flops 10000000000 | bytes 16777216 | tf_op jit(solution)/shard_map/pallas_call | solution.py:130
  272.8 3.3 %shard_map.461 = (f32[128,1024]{1,0:T(8,128)}, f32[128,1024]{1,0:T(8,128)}, f32[1,1024]{1,0:T(1,128)}, f32[96,1024]{1,0:T(8,128)}, f32[96,1024]{1,0:T(8,128)}, /...) custom-call(f32[128,1024]{1,0:T(8,128)} %get-tuple-element.102.refs_, ...), custom_call_target="tpu_custom_call" | custom-call | bytes 16777216 | tf_op jit(solution)/shard_map/pallas_call | solution.py:130
  (2 shorter events, 0.0 us)
where the time goes:
time: 279 us; the launch traced here: 276 us
  Pallas kernels  272 us (97%)
    pallas_call x4, Pallas kernels, run(): pl.pallas_call(kernel, out_shape=[jax.ShapeDtypeStruct(s, t) for _, s, t,...  272 us

commit v1 on v0

--- a/solution.py
+++ b/solution.py
@@ -30,6 +30,7 @@
 CHUNK = 64
 STEPS = ((0,), (1, 3), (2,))
 HALVES = ((1, 3), (2, 0))
+OTHERS = ((0, 1), (1, 0), (3, 0), (2, 0), (1, 1), (3, 1), (2, 1))
 GELU_C = math.sqrt(2.0 / math.pi)
 
 
@@ -57,13 +58,8 @@
     return {"mp": lax.rem(lax.axis_index("mp") + 16 + offset, 16)}
 
 
-def all_peers(window):
-    peers = [xc_peer(0, 1)] + [xc_peer(d, 0) for d in (1, 2, 3)]
-    if window:
-        return peers + [row_peer(o) for o in range(1, 16)]
-    for d in (1, 2, 3):
-        peers += [y_peer(d), z_peer(d)]
-    return peers
+def all_peers():
+    return [xc_peer(0, 1)] + [xc_peer(d, 0) for d in (1, 2, 3)] + [row_peer(o) for o in range(1, 16)]
 
 
 def greet(peers):
@@ -387,7 +383,7 @@
 def forward_body(r):
     x, c, y, z = place()
     mp = lax.axis_index("mp")
-    ready = greet(all_peers(True))
+    ready = greet(all_peers())
     net, loc = Net(r.send, r.recv), Local(r.sems)
 
     tokens = r.tok[...].astype(F32)
@@ -406,7 +402,10 @@
     r.pr[y, VEC + 5 : VEC + 6, 0:BW] = r.decay_shift[...]
     r.pr[y, VEC + 6 : VEC + 7, 0:BW] = r.input_shift[...]
     r.pr[y, VEC + 7 : VEC + 8, :] = jnp.ones((1, LANE), F32)
-    r.pr[y, VEC + 7 : VEC + 8, 0:BW] = r.softplus[...]
+    decay = r.decay_param[...]
+    r.pr[y, VEC + 7 : VEC + 8, 0:BW] = jnp.maximum(-decay, 0.0) + jnp.log1p(
+        jnp.exp(-jnp.abs(decay))
+    )
     ready()
     gather_n1 = spread_z(net, r.n1)
     half = pl.ds(pl.multiple_of(c * 512, 512), 512)
@@ -797,7 +796,7 @@
 def middle_body(r):
     _, _, _, z = place()
     mp = lax.axis_index("mp")
-    ready = greet(all_peers(True))
+    ready = greet(all_peers())
     net, loc = Net(r.send, r.recv), Local(r.sems)
     loads = {
         k: loc.load(getattr(r, "far_" + k), getattr(r, k))
@@ -833,12 +832,6 @@
     unit_grads(((r.dpg, r.n4), (r.dpu, r.n4), (r.hid, r.c_all)), r.gw2)
     reducer = Reducer(net, r.gw2, r, "red")
     reducer.start()
-    dn = r.own_d[...]
-    for d in (1, 3, 2):
-        back_d[d].wait_recv()
-        dn = dn + r.recv_d[d - 1].astype(F32)
-    dv, r.gg_four[...] = rms_back(dn, x, r.gain_four[...])
-    c = c + dv
 
     for ds in HALVES:
         slots = [(z + 4 - d) % 4 for d in ds]
@@ -849,6 +842,13 @@
             else:
                 r.part_o[d - 1] = block(term, i).astype(BF16)
                 back_o[d] = net.push(r.part_o.at[d - 1], r.recv_o.at[d - 1], z_peer(4 - d))
+
+    dn = r.own_d[...]
+    for d in (1, 3, 2):
+        back_d[d].wait_recv()
+        dn = dn + r.recv_d[d - 1].astype(F32)
+    dv, r.gg_four[...] = rms_back(dn, x, r.gain_four[...])
+    c = c + dv
 
     for k in ("wa", "kv", "pb", "q", "att", "n3", "x2"):
         loads[k].wait()
@@ -1007,12 +1007,11 @@
 def last_body(r):
     x, c, y, z = place()
     dp = lax.axis_index("dp")
-    ready = greet(all_peers(False) + [xc_peer(d, 1) for d in (1, 2, 3)])
+    ready = greet([xc_peer(*o) for o in OTHERS] + [row_peer(o) for o in range(1, 16)])
     net, loc = Net(r.send, r.recv), Local(r.sems)
-    attn_in = loc.load(r.far_gw_attn, r.gw_attn)
     loads = {
         k: loc.load(getattr(r, "far_" + k), getattr(r, k))
-        for k in ("w1", "pg", "pu", "c2_all", "n2", "wr", "gate", "state", "rate", "pr", "opened", "conv",
+        for k in ("c2_all", "w1", "pg", "pu", "gw_attn", "n2", "wr", "gate", "state", "rate", "pr", "opened", "conv",
                   "mix", "n1", "gated")
     }
     need = lambda *names: [loads[k].wait() for k in names]
@@ -1042,7 +1041,7 @@
                 r.part1[d - 1] = block(term, i).astype(BF16)
                 back[d] = net.push(r.part1.at[d - 1], r.recv1.at[d - 1], z_peer(4 - d))
         if ds == HALVES[0]:
-            attn_in.wait()
+            need("gw_attn")
             red_attn.start()
     red_attn.along_one()
     need("n2")
@@ -1180,12 +1179,6 @@
         r.du[SPAN : SPAN + 8, :] = jnp.zeros((8, CH), F32)
 
     red_first.along_two()
-    for b in range(4):
-        cols = slice(b * LANE, (b + 1) * LANE)
-        left = r.conv[:, b * LANE : b * LANE + BW]
-        r.gp[b, 0:BW, :] = low_dot(left, r.acum[:, cols], ((0,), (0,)))
-        r.gp[b, BW : 2 * BW, :] = low_dot(left, r.fac[:, cols], ((0,), (0,)))
-    red_a.along_one()
 
     @pl.when(y < 3)
     def _():
@@ -1225,7 +1218,13 @@
                 back[d] = net.push(r.part2.at[d - 1], r.recv2.at[d - 1], z_peer(4 - d))
             else:
                 r.grad_tokens[...] = block(term, i)
+    red_a.along_one()
     output_grads(r.gwb, 0, r.dpg, r.n1)
+    for b in range(4):
+        cols = slice(b * LANE, (b + 1) * LANE)
+        left = r.conv[:, b * LANE : b * LANE + BW]
+        r.gp[b, 0:BW, :] = low_dot(left, r.acum[:, cols], ((0,), (0,)))
+        r.gp[b, BW : 2 * BW, :] = low_dot(left, r.fac[:, cols], ((0,), (0,)))
     for b in range(4):
         cols = slice(b * LANE, (b + 1) * LANE)
         for k, row_sum in enumerate(sums + (dsp,)):
@@ -1261,7 +1260,7 @@
         cut = whole.at[dp]
         return [
             net.push(cut, cut, xc_peer(dx, dc))
-            for dx, dc in ((1, 0), (3, 0), (2, 0), (1, 1), (3, 1), (2, 1), (0, 1))
+            for dx, dc in OTHERS
         ]
 
     red_b.along_one()
@@ -1271,19 +1270,17 @@
         dn = dn + r.recv2[d - 1].astype(F32)
     dv, gg_one = rms_back(dn, r.tok[...].astype(F32), r.gain_one[...])
     r.grad_tokens[...] = r.c1[...] + dv
-    r.gains[...] = jnp.concatenate(
-        [gg_one, gg_two, r.gg_three[...], r.gg_four[...], jnp.zeros((4, D), F32)], axis=0
-    )
-    mine = spread(0, 0, [xc_peer(0, 1)])
+    for k, grad in enumerate((gg_one, gg_two, r.gg_three[...], r.gg_four[...])):
+        for j in range(8):
+            r.gains[k * 8 + j : k * 8 + j + 1, :] = grad[:, j * LANE : (j + 1) * LANE]
+    mine = spread(0, 0, [xc_peer(dx, dc) for dx, dc in OTHERS])
     shares = share(red_a, r.recur_a)
-    collect(0, mine)
-    mine = spread(1, 1, [xc_peer(d, 0) for d in (1, 3, 2)])
     red_b.along_two()
     a, b = red_first.finish()
     r.first_out[0:288, :] = a
     r.first_out[288:, :] = b
-    collect(1, mine)
-    mine = spread(2, 4, [y_peer(d) for d in (1, 3, 2)])
+    collect(0, mine)
+    mine = spread(1, 7, [row_peer(o) for o in range(1, 16)])
     shares += share(red_b, r.recur_b)
     total = r.z_out[z].astype(F32)
     for copy in z_in:
@@ -1291,8 +1288,6 @@
     for d in range(3):
         total = total + r.z_in[d].astype(F32)
     r.attn_out[...] = total
-    collect(4, mine)
-    mine = spread(3, 7, [z_peer(d) for d in (1, 3, 2)])
     collect(7, mine)
     for copy in shares:
         copy.wait_recv()
@@ -1308,7 +1303,7 @@
     ins += [("far_" + k, v, "far") for k, v in far.items()]
     outs = [
         ("grad_tokens", (ROWS, D), F32, "near"),
-        ("gains", (8, D), F32, "near"),
+        ("gains", (32, LANE), F32, "near"),
         ("first_out", (576, LANE), F32, "near"),
         ("attn_out", (16, PAIR), F32, "near"),
         ("recur_a", (8, 192, LANE), BF16, "near"),
@@ -1340,14 +1335,14 @@
         ("gp", vm((4, 256, LANE), F32)),
         ("gwa", vm((2, 4, 4, 192, LANE), BF16)),
         ("gwb", vm((2, 4, 4, 128, LANE), BF16)),
-        ("gain_in", vm((10, 8, D), F32)),
-        ("gain_out", vm((4, 8, D), F32)),
+        ("gain_in", vm((22, 32, LANE), F32)),
+        ("gain_out", vm((2, 32, LANE), F32)),
         *Reducer.scratch("rat", 64, PAIR),
         *Reducer.scratch("rff", 576, LANE),
         *Reducer.scratch("rea", 192, LANE),
         *Reducer.scratch("reb", 128, LANE),
-        ("send", dma(96)),
-        ("recv", dma(96)),
+        ("send", dma(112)),
+        ("recv", dma(112)),
         ("sems", dma(17)),
     ]
     return run(last_body, ins, outs, scratch, 3, 10**10)
@@ -1357,7 +1352,8 @@
     r.outputs[...] = r.in_outputs[...]
     r.tokens[...] = r.in_tokens[...]
     for i, name in enumerate(("norm_one", "norm_two", "norm_three", "norm_four")):
-        getattr(r, name)[...] = r.gains[i : i + 1, :]
+        for j in range(8):
+            getattr(r, name)[:, j * LANE : (j + 1) * LANE] = r.gains[i * 8 + j : i * 8 + j + 1, :]
     for part in range(8):
         rows = slice(part * LANE, (part + 1) * LANE)
         r.recur_gate[:, rows] = r.recur_a[part, 0:BW, :].astype(F32)
@@ -1370,7 +1366,8 @@
     r.conv_bias[...] = params[VEC + 4 : VEC + 5, :BW]
     r.decay_shift[...] = params[VEC + 5 : VEC + 6, :BW]
     r.input_shift[...] = params[VEC + 6 : VEC + 7, :BW]
-    r.decay_param[...] = params[VEC + 7 : VEC + 8, :BW] * r.slope[...]
+    slope = -jax.nn.sigmoid(-r.decay[...])
+    r.decay_param[...] = params[VEC + 7 : VEC + 8, :BW] * slope
     for name in ("first", "second"):
         summed = getattr(r, name)
         getattr(r, name + "_gate")[...] = summed[0:192, :]
@@ -1428,7 +1425,7 @@
             gain_four=gain_four, recur_input=recur_input.T, recur_gate=recur_gate.T, recur_output=recur_output,
             conv_kernel=conv_kernel, conv_bias=flat(conv_bias), decay_gate=decay_gate,
             decay_shift=flat(decay_shift), input_gate=input_gate,
-            input_shift=flat(input_shift), softplus=flat(jax.nn.softplus(-decay_param)),
+            input_shift=flat(input_shift), decay_param=flat(decay_param),
             first_gate=first_gate.T, first_value=first_value.T, first_down=first_down,
             query_proj=query_proj, key_proj=key_proj, value_proj=value_proj,
             attn_output=attn_output, second_gate=second_gate.T, second_value=second_value.T,
@@ -1468,7 +1465,7 @@
             ("first", end["first_out"], "near"),
             ("second", mid["second_out"], "near"),
             ("attn", end["attn_out"], "near"),
-            ("slope", flat(-jax.nn.sigmoid(-decay_param)), "near"),
+            ("decay", flat(decay_param), "near"),
         ],
         [(name, shape, F32, "near") for name, shape in OUTPUTS],
         [],

time: 279 us -> 275 us (0.986)
  Pallas kernels: 272 us -> 269 us
    pallas_call x4, Pallas kernels: 272 us -> 269 us  [run(): pl.pallas_call(kernel, out_shape=[jax.ShapeDtypeStruct(s, t) for _, s, t,...]
where the time goes in v1:
time: 275 us; the launch traced here: 272 us
  Pallas kernels  269 us (98%)
    pallas_call x4, Pallas kernels, run(): pl.pallas_call(kernel, out_shape=[jax.ShapeDtypeStruct(s, t) for _, s, t,...  269 us

profile of v1, /device:TPU:0, one launch (start us, length us, event | category | flops | bytes accessed | tf_op | source)
XLA Modules:
  0.0 272.1 jit_solution(8310891301628577957)
XLA Ops:
  1.3 0.5 broadcast_in_dim.10.refs_2_.refs_3_
  1.9 0.3 fusion
  2.2 0.8 pad_maximum_fusion
  2.9 106.5 %shard_map.458 = (bf16[4,128,1024]{2,1,0:T(8,128)(2,1)}, bf16[3,512,1024]{2,1,0:T(8,128)(2,1)}, f32[4,208,128]{2,1,0:T(8,128)}, f32[520,512]{1,0:T(8,128)}, f32[...) custom-call(bf16[128,1024]{1,0:T(8,128)(2,1)} %refs_2_.1, ...), custom_call_target="tpu_custom_call" | custom-call | flops 10000000000 | bytes 16777216 | tf_op jit(solution)/shard_map/pallas_call | solution.py:126
  109.5 68.0 %shard_map.459 = (f32[128,1024]{1,0:T(8,128)}, f32[128,1024]{1,0:T(8,128)}, f32[1,1024]{1,0:T(1,128)}, f32[1,1024]{1,0:T(1,128)}, f32[576,128]{1,0:T(8,128)}, /*...) custom-call(f32[128,1024]{1,0:T(8,128)} %get-tuple-element.91.refs_0_, bf16[128,1024]{1,0:T(8,128)(2,1)} %refs_1_.3, ...), custom_call_target="tpu_custom_call" | custom-call | flops 10000000000 | bytes 16777216 | tf_op jit(solution)/shard_map/pallas_call | solution.py:126
  177.4 91.1 %shard_map.460 = (f32[128,1024]{1,0:T(8,128)}, f32[32,128]{1,0:T(8,128)}, f32[576,128]{1,0:T(8,128)}, f32[16,1152]{1,0:T(8,128)}, bf16[8,192,128]{2,1,0:T(8,128)(2,1)}, /*index=5*/bf16[8,128,128]{2,1,0:T(8,128)(2,1)}) custom-call(f32[128,1024]{1,0:T(8,128)} %get-tuple-element.103.refs_0_, f32[128,1024]{1,0:T(8,128)} %get-tuple-element.104.refs_1_, ...), custom_call_target="tpu_custom_call" | custom-call | flops 10000000000 | bytes 16777216 | tf_op jit(solution)/shard_map/pallas_call | solution.py:126
  268.5 3.3 %shard_map.461 = (f32[128,1024]{1,0:T(8,128)}, f32[128,1024]{1,0:T(8,128)}, f32[1,1024]{1,0:T(1,128)}, f32[96,1024]{1,0:T(8,128)}, f32[96,1024]{1,0:T(8,128)}, /...) custom-call(f32[128,1024]{1,0:T(8,128)} %get-tuple-element.102.refs_, ...), custom_call_target="tpu_custom_call" | custom-call | bytes 16777216 | tf_op jit(solution)/shard_map/pallas_call | solution.py:126
  (2 shorter events, 0.0 us)
